TPU v7x, 512 devices: a whole 4x8x8 slice. The times are simulated.
512 devices in a mesh: dp: 16 (over y_lo, x, core), seq: 32 (over y_hi, z).
Axes of the slice: x: 4, y: 8 (y_hi: 4, y_lo: 2; y = y_hi * 2 + y_lo), z: 8, core: 2. Of those that a mesh axis runs over, the one named last changes fastest.
Arguments:
- query_raw: bfloat16 [32, 16, 2048, 128], P('dp', None, 'seq'), may hold values from -6 to 6
- key_raw: bfloat16 [32, 16, 2048, 128], P('dp', None, 'seq'), may hold values from -6 to 6
- values: bfloat16 [32, 16, 2048, 128], P('dp', None, 'seq'), may hold values from -6 to 6
- residuals: bfloat16 [3, 32, 16, 2048, 128], P(None, 'dp', None, 'seq'), may hold values from -6 to 6
- block_section: int32 [3], replicated, may hold values from 0 to 31
- gain_query: float32 [128], replicated, may hold values from 0.5 to 2
- gain_key: float32 [128], replicated, may hold values from 0.5 to 2
Outputs:
- grad_query: bfloat16 [32, 16, 2048, 128], P('dp', None, 'seq')
- grad_key: bfloat16 [32, 16, 2048, 128], P('dp', None, 'seq')
- grad_values: bfloat16 [32, 16, 2048, 128], P('dp', None, 'seq')
- grad_gains: float32 [256], P('dp')
Inputs may be any that keep to these rules, and one draw needn't show every extreme that they name: `block_section`: section indices.
All inputs are finite; a program needn't handle non-finite values.
Results may differ from a plain program's by a relative error of at most 0.012.
The roundings to bfloat16 on the way count: a program that leaves them out, or rounds other values in their place, can miss the bound.
Values may be sent and summed in bfloat16 or wider, within the bound.
A program may use at most 64 MiB of HBM per device.

v0:
```python
import functools
import math

import jax
import jax.numpy as jnp
from jax import lax
from jax.experimental import pallas as pl
from jax.experimental.pallas import tpu as pltpu
from jax.sharding import PartitionSpec as P

MESH = pl.DeviceIdType.MESH
epsilon = 1e-06
NY, NZ = 4, 8
QB = 256
KT = 512
BF, F32 = jnp.bfloat16, jnp.float32


def dot(a, b, dims):
    return lax.dot_general(a, b, (dims, ((), ())), preferred_element_type=F32)


def normalize(entries):
    inverse = lax.rsqrt(jnp.mean(entries * entries, axis=-1, keepdims=True) + epsilon)
    return entries * inverse, inverse


def restore(unit, inverse, grad_norm, gain):
    grad_unit = grad_norm * gain
    return inverse * (grad_unit - unit * jnp.mean(grad_unit * unit, axis=-1, keepdims=True))


def kernel(
    sec, gain_q, gain_k, q_in, k_in, v_in, r_in,
    q_out, k_out, v_out, g_out,
    k_mid, v_mid, q_mid, r_mid0, r_mid1, r_mid2, r_mid3,
    k_land, v_land, q_land, r_land0, r_land1, r_land2, r_land3,
    kn, knt, do_f, do_b, e_buf, dp_buf, dk_acc, dv_acc,
    dq_stage, dk_stage, dv_stage, dq_mid, dk_mid_a, dk_mid_b, dv_mid,
    g_part, g_z, g_y, g_d,
    sem1, sem2, send1, send2, gsem, gsend,
):
    me = lax.axis_index("seq")
    dp = lax.axis_index("dp")
    y, z = me // NZ, me % NZ
    scale = 128 ** (-0.5)
    r_mid = (r_mid0, r_mid1, r_mid2, r_mid3)
    r_land = (r_land0, r_land1, r_land2, r_land3)
    n_dp = g_d.shape[0]

    def at_z(dz):
        return {"seq": y * NZ + (z + dz) % NZ}

    def at_y(dy):
        return {"seq": ((y + dy) % NY) * NZ + z}

    barrier = pltpu.get_barrier_semaphore()
    for dz in range(1, NZ):
        pl.semaphore_signal(barrier, 1, device_id=at_z(dz), device_id_type=MESH)
    for dy in range(1, NY):
        pl.semaphore_signal(barrier, 1, device_id=at_y(dy), device_id_type=MESH)
    for dd in range(1, n_dp):
        pl.semaphore_signal(barrier, 1, device_id={"dp": (dp + dd) % n_dp}, device_id_type=MESH)
    pl.semaphore_wait(barrier, NZ - 1 + NY - 1 + n_dp - 1)

    def local(src, dst, sem):
        pltpu.make_async_copy(src, dst, sem).start()

    def remote(src, dst, send, recv, device):
        pltpu.make_async_remote_copy(
            src_ref=src, dst_ref=dst, send_sem=send, recv_sem=recv, device_id=device, device_id_type=MESH
        ).start()

    def wait(ref, sem):
        pltpu.make_async_copy(ref, ref, sem).wait()

    zo = (4, 3, 5, 2, 6, 1, 7)
    yo = (2, 1, 3)

    def first(n, path, src, mid):
        if path == "a":
            local(src.at[:, z], mid.at[z], sem1.at[n])
            for dz in zo:
                remote(src.at[:, (z + dz) % NZ], mid.at[z], send1.at[n], sem1.at[n], at_z(dz))
        else:
            local(src.at[y], mid.at[y], sem1.at[n])
            for dy in yo:
                remote(src.at[(y + dy) % NY], mid.at[y], send1.at[n], sem1.at[n], at_y(dy))

    def second(n, path, mid, land):
        wait(mid, sem1.at[n])
        if path == "a":
            local(mid.at[:, y], land.at[y], sem2.at[n])
            for dy in yo:
                remote(mid.at[:, (y + dy) % NY], land.at[y], send2.at[n], sem2.at[n], at_y(dy))
        else:
            local(mid.at[:, z], land.at[:, z], sem2.at[n])
            for dz in zo:
                remote(mid.at[:, (z + dz) % NZ], land.at[:, z], send2.at[n], sem2.at[n], at_z(dz))

    def sent(n, path, mid):
        if path == "a":
            wait(mid.at[pl.ds(0, NZ - 1)], send1.at[n])
            wait(mid.at[:, pl.ds(0, NY - 1)], send2.at[n])
        else:
            wait(mid.at[pl.ds(0, NY - 1)], send1.at[n])
            wait(mid.at[:, pl.ds(0, NZ - 1)], send2.at[n])

    low, high = pl.ds(0, 32), pl.ds(32, 32)
    streams = [
        ("a", k_in, k_mid, k_land),
        ("b", v_in, v_mid, v_land),
        ("a", q_in.at[:, :, low], q_mid.at[0].reshape(NZ, NY, 32, 128), q_land.at[:, :, low]),
        ("b", q_in.at[:, :, high], q_mid.at[1].reshape(NY, NZ, 32, 128), q_land.at[:, :, high]),
    ]
    for c in range(4):
        for i in range(3):
            path = ("a", "b", "ab"[c % 2])[i]
            shape = (NZ, NY, 16, 128) if path == "a" else (NY, NZ, 16, 128)
            streams.append(
                (path, r_in.at[i, :, :, pl.ds(16 * c, 16)], r_mid[c].at[i].reshape(*shape), r_land[c].at[i])
            )
    n_in = len(streams)

    for n, (path, src, mid, land) in enumerate(streams):
        first(n, path, src, mid)
    for n, (path, src, mid, land) in enumerate(streams):
        second(n, path, mid, land)

    wait(k_land, sem2.at[0])
    for t in range(NY):
        unit, _ = normalize(k_land[t].reshape(512, 128).astype(F32))
        norm = unit * gain_k[...]
        kn[pl.ds(512 * t, 512), :] = norm.astype(BF)
        knt[:, pl.ds(512 * t, 512)] = norm.T.astype(BF)
    dk_acc[...] = jnp.zeros_like(dk_acc)
    dv_acc[...] = jnp.zeros_like(dv_acc)
    wait(v_land, sem2.at[1])
    wait(q_land.at[:, :, low], sem2.at[2])
    wait(q_land.at[:, :, high], sem2.at[3])

    def queries(c, b, part_q):
        raw = q_land[c, pl.ds(4 * b, 4)].reshape(QB, 128).astype(F32)
        unit, inverse = normalize(raw)
        qn = (unit * gain_q[...]).astype(BF)
        go = do_b[pl.ds(pl.multiple_of(QB * b, QB), QB), :]

        def one(t, carry):
            total, mixed = carry
            keys = pl.ds(pl.multiple_of(KT * t, KT), KT)
            weights = jnp.exp2(dot(kn[keys, :], qn, ((1,), (1,))) * (scale * math.log2(math.e)))
            grad_probs = dot(v_land[t].reshape(KT, 128), go, ((1,), (1,)))
            e_buf[keys, :] = weights
            dp_buf[keys, :] = grad_probs
            return (
                total + jnp.sum(weights, axis=0, keepdims=True),
                mixed + jnp.sum(weights * grad_probs, axis=0, keepdims=True),
            )

        zero = jnp.zeros((1, QB), F32)
        total, mixed = lax.fori_loop(0, 2048 // KT, one, (zero, zero))
        over = 1.0 / total
        centre = mixed * over

        def two(t, dqt):
            keys = pl.ds(pl.multiple_of(KT * t, KT), KT)
            probs = e_buf[keys, :] * over
            grad_scores = (probs * (dp_buf[keys, :] - centre)).astype(BF)
            dk_acc[keys, :] += dot(grad_scores, qn, ((1,), (0,)))
            dv_acc[keys, :] += dot(probs.astype(BF), go, ((1,), (0,)))
            return dqt + dot(knt[:, keys], grad_scores, ((1,), (0,)))

        dqt = lax.fori_loop(0, 2048 // KT, two, jnp.zeros((128, QB), F32))
        grad_norm = dqt.T * scale
        out = restore(unit, inverse, grad_norm, gain_q[...]).astype(BF)
        dq_stage[c, pl.ds(4 * b, 4)] = out.reshape(4, 64, 128)
        return part_q + jnp.sum(grad_norm * unit, axis=0, keepdims=True)

    n_dq = n_in

    def send_dq(c):
        local(dq_stage.at[c, z], dq_mid.at[z, c], sem1.at[n_dq])
        for dz in zo:
            remote(
                dq_stage.at[c, (z + dz) % NZ], dq_mid.at[z, c], send1.at[n_dq], sem1.at[n_dq], at_z(dz)
            )

    part_q = jnp.zeros((1, 128), F32)
    for c in range(4):
        for i in range(3):
            wait(r_land[c].at[i], sem2.at[4 + 3 * c + i])
        if c == 3:
            for done in range(3):
                send_dq(done)
        for r in range(32):
            total = None
            for i in range(3):
                d = (r + 32 - sec[i]) % 32
                row = r_land[c][i, d // NZ, d % NZ].astype(F32)
                total = row if total is None else total + row
            do_f[:, r, :] = total
        do_b[...] = do_f[...].reshape(512, 128).astype(BF)
        part_q = lax.fori_loop(0, 2, lambda b, p, c=c: queries(c, b, p), part_q)
    send_dq(3)

    for t in range(NY):
        dv_stage[t] = dv_acc[pl.ds(512 * t, 512), :].astype(BF).reshape(NZ, 64, 128)
    n_dv, n_dka, n_dkb = n_in + 1, n_in + 2, n_in + 3
    first(n_dv, "b", dv_stage, dv_mid)
    part_k = jnp.zeros((1, 128), F32)
    for t in range(NY):
        unit, inverse = normalize(k_land[t].reshape(512, 128).astype(F32))
        grad_norm = dk_acc[pl.ds(512 * t, 512), :] * scale
        part_k = part_k + jnp.sum(grad_norm * unit, axis=0, keepdims=True)
        out = restore(unit, inverse, grad_norm, gain_k[...]).astype(BF)
        dk_stage[t] = out.reshape(NZ, 64, 128)

    g_part[0, :, :] = jnp.concatenate([part_q, part_k, jnp.zeros((6, 128), F32)], axis=0)
    local(g_part.at[0], g_z.at[z], gsem.at[0])
    for dz in zo:
        remote(g_part.at[0], g_z.at[z], gsend.at[0], gsem.at[0], at_z(dz))

    first(n_dka, "a", dk_stage.at[:, :, low], dk_mid_a)
    first(n_dkb, "b", dk_stage.at[:, :, high], dk_mid_b)

    wait(g_z, gsem.at[0])
    g_part[1, :, :] = jnp.sum(g_z[...], axis=0)
    local(g_part.at[1], g_y.at[y], gsem.at[1])
    for dy in yo:
        remote(g_part.at[1], g_y.at[y], gsend.at[1], gsem.at[1], at_y(dy))

    second(n_dq, "a", dq_mid, q_out)

    wait(g_y, gsem.at[1])
    g_part[2, :, :] = jnp.sum(g_y[...], axis=0)
    local(g_part.at[2], g_d.at[dp], gsem.at[2])
    for dd in range(1, n_dp):
        remote(g_part.at[2], g_d.at[dp], gsend.at[2], gsem.at[2], {"dp": (dp + dd) % n_dp})

    second(n_dv, "b", dv_mid, v_out)
    second(n_dka, "a", dk_mid_a, k_out.at[:, :, low])
    second(n_dkb, "b", dk_mid_b, k_out.at[:, :, high])

    wait(g_d, gsem.at[2])
    g_out[...] = jnp.sum(g_d[...], axis=0)

    for n, (path, src, mid, land) in enumerate(streams):
        sent(n, path, mid)
    sent(n_dq, "a", dq_mid)
    sent(n_dv, "b", dv_mid)
    sent(n_dka, "a", dk_mid_a)
    sent(n_dkb, "b", dk_mid_b)
    wait(g_z.at[pl.ds(0, NZ - 1)], gsend.at[0])
    wait(g_y.at[pl.ds(0, NY - 1)], gsend.at[1])
    wait(g_d.at[pl.ds(0, n_dp - 1)], gsend.at[2])
    wait(q_out, sem2.at[n_dq])
    wait(v_out, sem2.at[n_dv])
    wait(k_out.at[:, :, low], sem2.at[n_dka])
    wait(k_out.at[:, :, high], sem2.at[n_dkb])


def on_device(query_raw, key_raw, values, residuals, block_section, gain_query, gain_key):
    n_dp = lax.axis_size("dp")
    local_shape = query_raw.shape
    grid = (NY, NZ, 64, 128)
    vmem, dma = pltpu.VMEM, pltpu.SemaphoreType.DMA
    block = functools.partial(vmem, dtype=BF)
    full = jax.ShapeDtypeStruct(grid, BF)
    scratch = [
        vmem((NZ, NY, 64, 128), BF), vmem(grid, BF), vmem((2, 32, 32, 128), BF),
        *[vmem((3, 32, 16, 128), BF)] * 4,
        vmem(grid, BF), vmem(grid, BF), vmem(grid, BF),
        *[vmem((3, NY, NZ, 16, 128), BF)] * 4,
        vmem((2048, 128), BF), vmem((128, 2048), BF),
        vmem((16, 32, 128), F32), vmem((512, 128), BF),
        vmem((2048, QB), F32), vmem((2048, QB), F32),
        vmem((2048, 128), F32), vmem((2048, 128), F32),
        vmem(grid, BF), vmem(grid, BF), vmem(grid, BF),
        vmem((NZ, NY, 64, 128), BF), vmem((NZ, NY, 32, 128), BF), vmem((NY, NZ, 32, 128), BF), vmem(grid, BF),
        vmem((3, 8, 128), F32), vmem((NZ, 8, 128), F32), vmem((NY, 8, 128), F32), vmem((n_dp, 8, 128), F32),
        dma((20,)), dma((20,)), dma((20,)), dma((20,)), dma((3,)), dma((3,)),
    ]
    anywhere = pl.BlockSpec(memory_space=pl.ANY)
    inside = pl.BlockSpec(memory_space=pltpu.VMEM)
    grad_q, grad_k, grad_v, gains = pl.pallas_call(
        kernel,
        out_shape=(full, full, full, jax.ShapeDtypeStruct((8, 128), F32)),
        in_specs=[pl.BlockSpec(memory_space=pltpu.SMEM), inside, inside] + [anywhere] * 4,
        out_specs=(anywhere, anywhere, anywhere, inside),
        scratch_shapes=scratch,
        compiler_params=pltpu.CompilerParams(
            collective_id=0, has_side_effects=True, vmem_limit_bytes=48 << 20
        ),
        name="attention_backward",
    )(
        block_section,
        gain_query.reshape(1, 128),
        gain_key.reshape(1, 128),
        query_raw.reshape(grid),
        key_raw.reshape(grid),
        values.reshape(grid),
        residuals.reshape((3,) + grid),
    )
    share = 256 // n_dp
    grad_gains = lax.dynamic_slice(gains.reshape(-1), (lax.axis_index("dp") * share,), (share,))
    return (
        grad_q.reshape(local_shape),
        grad_k.reshape(local_shape),
        grad_v.reshape(local_shape),
        grad_gains,
    )


def solution(mesh):
    placed = (
        P("dp", None, "seq", None),
        P("dp", None, "seq", None),
        P("dp", None, "seq", None),
        P(None, "dp", None, "seq", None),
        P(),
        P(),
        P(),
    )
    return jax.shard_map(
        on_device,
        mesh=mesh,
        in_specs=placed,
        out_specs=(
            P("dp", None, "seq", None),
            P("dp", None, "seq", None),
            P("dp", None, "seq", None),
            P("dp"),
        ),
        check_vma=False,
    )
```

profile of v0, /device:TPU:5, one launch (start us, length us, event | category | flops | bytes accessed | tf_op | source)
XLA Modules:
  0.0 158.8 jit_solution(14144106993764902878)
XLA Ops:
  0.6 0.0 copy-start
  0.6 1.4 copy-done
  2.0 0.0 copy-start.1
  2.0 1.0 copy-done.1
  3.1 0.0 copy-start.2
  3.1 1.0 copy-done.2
  4.1 0.0 copy-start.3
  4.1 1.0 copy-done.3
  5.2 0.0 copy-start.4
  5.2 0.7 copy-done.4
  5.8 0.0 copy-start.5
  5.8 0.7 copy-done.5
  6.5 0.0 copy-start.6
  6.5 0.7 copy-done.6
  7.1 148.7 %attention_backward.1 = (bf16[4,8,64,128]{3,2,1,0:T(8,128)(2,1)S(1)}, bf16[4,8,64,128]{3,2,1,0:T(8,128)(2,1)S(1)}, bf16[4,8,64,128]{3,2,1,0:T(8,128)(2,1)S(1)}, f32[8,128]{1,0:T(8,128)S(1)}) custom-call(s32[3]{0:T(128)S(1)} %copy-done.4, f32[1,128]{1,0:T(1,128)S(1)} %bitcast.17, f32[1,128]{1,0:T(1,128)S(1)} %bitcast.18, ...), custom_call_target="tpu_custom_call" | custom-call | tf_op jit(solution)/shard_map/attention_backward/pallas_call | solution.py:285
  155.8 0.6 dynamic_slice.3
  156.4 0.8 copy.14
  157.2 0.8 copy.15
  158.0 0.8 copy.16
Async XLA Ops:
  0.6 1.4 copy-start
  2.0 1.0 copy-start.1
  3.1 1.0 copy-start.2
  4.1 1.0 copy-start.3
  5.2 0.7 copy-start.4
  5.8 0.7 copy-start.5
  6.5 0.7 copy-start.6
where the time goes:
time: 159 us
  Pallas kernels  149 us (94%)
  local copies, waits for them, and re-layouts  9.46 us (6%)
    pallas_call x1, Pallas kernels, on_device(): pl.pallas_call(kernel, out_shape=(full, full, full, jax.ShapeDtypeStruct(...  149 us
    unnamed x17, local copies, waits for them, and re-layouts  8.87 us

commit v1 on v0

--- a/solution.py
+++ b/solution.py
@@ -1,4 +1,3 @@
-import functools
 import math
 
 import jax
@@ -11,8 +10,7 @@
 MESH = pl.DeviceIdType.MESH
 epsilon = 1e-06
 NY, NZ = 4, 8
-QB = 256
-KT = 512
+QB = 512
 BF, F32 = jnp.bfloat16, jnp.float32
 
 
@@ -31,14 +29,14 @@
 
 
 def kernel(
-    sec, gain_q, gain_k, q_in, k_in, v_in, r_in,
+    sec_in, gain_q_in, gain_k_in, q_in, k_in, v_in, r_in,
     q_out, k_out, v_out, g_out,
     k_mid, v_mid, q_mid, r_mid0, r_mid1, r_mid2, r_mid3,
     k_land, v_land, q_land, r_land0, r_land1, r_land2, r_land3,
-    kn, knt, do_f, do_b, e_buf, dp_buf, dk_acc, dv_acc,
-    dq_stage, dk_stage, dv_stage, dq_mid, dk_mid_a, dk_mid_b, dv_mid,
-    g_part, g_z, g_y, g_d,
-    sem1, sem2, send1, send2, gsem, gsend,
+    kn, qn, do_f, probs, probs_b, mixed, dk_acc, dv_acc,
+    dq_stage, dk_stage, dv_stage, dq_mid_a, dq_mid_b, dk_mid_a, dk_mid_b, dv_mid,
+    g_part, g_z, g_y, g_d, sec, gain_q, gain_k,
+    sem1, sem2, send1, send2, gsem, gsend, own,
 ):
     me = lax.axis_index("seq")
     dp = lax.axis_index("dp")
@@ -124,88 +122,98 @@
 
     for n, (path, src, mid, land) in enumerate(streams):
         first(n, path, src, mid)
+    small = ((sec_in, sec), (gain_q_in, gain_q), (gain_k_in, gain_k))
+    for n, (src, dst) in enumerate(small):
+        local(src, dst, own.at[n])
     for n, (path, src, mid, land) in enumerate(streams):
         second(n, path, mid, land)
+    for n, (src, dst) in enumerate(small):
+        pltpu.make_async_copy(src, dst, own.at[n]).wait()
 
     wait(k_land, sem2.at[0])
     for t in range(NY):
         unit, _ = normalize(k_land[t].reshape(512, 128).astype(F32))
-        norm = unit * gain_k[...]
-        kn[pl.ds(512 * t, 512), :] = norm.astype(BF)
-        knt[:, pl.ds(512 * t, 512)] = norm.T.astype(BF)
+        kn[pl.ds(512 * t, 512), :] = (unit * gain_k[...]).astype(BF)
     dk_acc[...] = jnp.zeros_like(dk_acc)
     dv_acc[...] = jnp.zeros_like(dv_acc)
     wait(v_land, sem2.at[1])
     wait(q_land.at[:, :, low], sem2.at[2])
     wait(q_land.at[:, :, high], sem2.at[3])
 
-    def queries(c, b, part_q):
-        raw = q_land[c, pl.ds(4 * b, 4)].reshape(QB, 128).astype(F32)
-        unit, inverse = normalize(raw)
-        qn = (unit * gain_q[...]).astype(BF)
-        go = do_b[pl.ds(pl.multiple_of(QB * b, QB), QB), :]
-
-        def one(t, carry):
-            total, mixed = carry
-            keys = pl.ds(pl.multiple_of(KT * t, KT), KT)
-            weights = jnp.exp2(dot(kn[keys, :], qn, ((1,), (1,))) * (scale * math.log2(math.e)))
-            grad_probs = dot(v_land[t].reshape(KT, 128), go, ((1,), (1,)))
-            e_buf[keys, :] = weights
-            dp_buf[keys, :] = grad_probs
-            return (
-                total + jnp.sum(weights, axis=0, keepdims=True),
-                mixed + jnp.sum(weights * grad_probs, axis=0, keepdims=True),
-            )
-
-        zero = jnp.zeros((1, QB), F32)
-        total, mixed = lax.fori_loop(0, 2048 // KT, one, (zero, zero))
-        over = 1.0 / total
-        centre = mixed * over
-
-        def two(t, dqt):
-            keys = pl.ds(pl.multiple_of(KT * t, KT), KT)
-            probs = e_buf[keys, :] * over
-            grad_scores = (probs * (dp_buf[keys, :] - centre)).astype(BF)
-            dk_acc[keys, :] += dot(grad_scores, qn, ((1,), (0,)))
-            dv_acc[keys, :] += dot(probs.astype(BF), go, ((1,), (0,)))
-            return dqt + dot(knt[:, keys], grad_scores, ((1,), (0,)))
-
-        dqt = lax.fori_loop(0, 2048 // KT, two, jnp.zeros((128, QB), F32))
-        grad_norm = dqt.T * scale
-        out = restore(unit, inverse, grad_norm, gain_q[...]).astype(BF)
-        dq_stage[c, pl.ds(4 * b, 4)] = out.reshape(4, 64, 128)
-        return part_q + jnp.sum(grad_norm * unit, axis=0, keepdims=True)
-
-    n_dq = n_in
+    def before(c, carry):
+        unit, _ = normalize(q_land[c].reshape(QB, 128).astype(F32))
+        norm = (unit * gain_q[...]).astype(BF)
+        qn[c] = norm
+        weights = jnp.exp2(dot(kn[...], norm, ((1,), (1,))) * (scale * math.log2(math.e)))
+        probs[c] = weights
+        over = 1.0 / jnp.sum(weights, axis=0, keepdims=True)
+        share = probs[c] * over
+        upper = share.astype(BF)
+        lower = (share - upper.astype(F32)).astype(BF)
+        probs[c] = share
+        probs_b[c] = upper
+        held = v_land[...].reshape(2048, 128)
+        mixed[c] = dot(held, upper, ((0,), (0,))) + dot(held, lower, ((0,), (0,)))
+        return carry
+
+    lax.fori_loop(0, 4, before, 0)
+
+    n_dqa, n_dqb, n_dv, n_dka, n_dkb = range(n_in, n_in + 5)
 
     def send_dq(c):
-        local(dq_stage.at[c, z], dq_mid.at[z, c], sem1.at[n_dq])
+        local(dq_stage.at[c, z, low], dq_mid_a.at[z, c], sem1.at[n_dqa])
         for dz in zo:
             remote(
-                dq_stage.at[c, (z + dz) % NZ], dq_mid.at[z, c], send1.at[n_dq], sem1.at[n_dq], at_z(dz)
+                dq_stage.at[c, (z + dz) % NZ, low], dq_mid_a.at[z, c],
+                send1.at[n_dqa], sem1.at[n_dqa], at_z(dz),
             )
 
-    part_q = jnp.zeros((1, 128), F32)
-    for c in range(4):
-        for i in range(3):
-            wait(r_land[c].at[i], sem2.at[4 + 3 * c + i])
-        if c == 3:
-            for done in range(3):
-                send_dq(done)
-        for r in range(32):
-            total = None
-            for i in range(3):
-                d = (r + 32 - sec[i]) % 32
-                row = r_land[c][i, d // NZ, d % NZ].astype(F32)
-                total = row if total is None else total + row
-            do_f[:, r, :] = total
-        do_b[...] = do_f[...].reshape(512, 128).astype(BF)
-        part_q = lax.fori_loop(0, 2, lambda b, p, c=c: queries(c, b, p), part_q)
+        @pl.when(y == c)
+        def _():
+            local(dq_stage.at[c, :, high], dq_mid_b.at[y], sem1.at[n_dqb])
+
+        @pl.when(y != c)
+        def _():
+            remote(
+                dq_stage.at[c, :, high], dq_mid_b.at[y],
+                send1.at[n_dqb], sem1.at[n_dqb], {"seq": c * NZ + z},
+            )
+
+    def after(c, part_q):
+        for cc in range(4):
+
+            @pl.when(c == cc)
+            def _():
+                for i in range(3):
+                    wait(r_land[cc].at[i], sem2.at[4 + 3 * cc + i])
+                if cc == 3:
+                    for done in range(3):
+                        send_dq(done)
+                for r in range(32):
+                    total = None
+                    for i in range(3):
+                        d = (r + 32 - sec[i]) % 32
+                        row = r_land[cc][i, d // NZ, d % NZ].astype(F32)
+                        total = row if total is None else total + row
+                    do_f[pl.ds(r, 16, stride=32), :] = total
+
+        grad_out = do_f[...].astype(BF)
+        centre = jnp.sum(grad_out.astype(F32).T * mixed[c], axis=0, keepdims=True)
+        grad_probs = dot(v_land[...].reshape(2048, 128), grad_out, ((1,), (1,)))
+        grad_scores = (probs[c] * (grad_probs - centre)).astype(BF)
+        dk_acc[...] += dot(grad_scores, qn[c], ((1,), (0,)))
+        dv_acc[...] += dot(probs_b[c], grad_out, ((1,), (0,)))
+        grad_norm = dot(kn[...], grad_scores, ((0,), (0,))).T * scale
+        unit, inverse = normalize(q_land[c].reshape(QB, 128).astype(F32))
+        out = restore(unit, inverse, grad_norm, gain_q[...]).astype(BF)
+        dq_stage[c] = out.reshape(NZ, 64, 128)
+        return part_q + jnp.sum(grad_norm * unit, axis=0, keepdims=True)
+
+    part_q = lax.fori_loop(0, 4, after, jnp.zeros((1, 128), F32))
     send_dq(3)
 
     for t in range(NY):
         dv_stage[t] = dv_acc[pl.ds(512 * t, 512), :].astype(BF).reshape(NZ, 64, 128)
-    n_dv, n_dka, n_dkb = n_in + 1, n_in + 2, n_in + 3
     first(n_dv, "b", dv_stage, dv_mid)
     part_k = jnp.zeros((1, 128), F32)
     for t in range(NY):
@@ -229,7 +237,8 @@
     for dy in yo:
         remote(g_part.at[1], g_y.at[y], gsend.at[1], gsem.at[1], at_y(dy))
 
-    second(n_dq, "a", dq_mid, q_out)
+    second(n_dqa, "a", dq_mid_a, q_out.at[:, :, low])
+    second(n_dqb, "b", dq_mid_b, q_out.at[:, :, high])
 
     wait(g_y, gsem.at[1])
     g_part[2, :, :] = jnp.sum(g_y[...], axis=0)
@@ -242,21 +251,41 @@
     second(n_dkb, "b", dk_mid_b, k_out.at[:, :, high])
 
     wait(g_d, gsem.at[2])
-    g_out[...] = jnp.sum(g_d[...], axis=0)
+    sums = jnp.sum(g_d[...], axis=0)
+    per_row = 128 * n_dp // 256
+    row = jnp.where(dp // per_row == 0, sums[0:1], sums[1:2])
+    start = (dp % per_row) * (256 // n_dp)
+    g_out[...] = pltpu.roll(jnp.broadcast_to(row, (8, 128)), (128 - start) % 128, 1)
 
     for n, (path, src, mid, land) in enumerate(streams):
         sent(n, path, mid)
-    sent(n_dq, "a", dq_mid)
+    sent(n_dqa, "a", dq_mid_a)
+    sent(n_dqb, "b", dq_mid_b)
     sent(n_dv, "b", dv_mid)
     sent(n_dka, "a", dk_mid_a)
     sent(n_dkb, "b", dk_mid_b)
     wait(g_z.at[pl.ds(0, NZ - 1)], gsend.at[0])
     wait(g_y.at[pl.ds(0, NY - 1)], gsend.at[1])
     wait(g_d.at[pl.ds(0, n_dp - 1)], gsend.at[2])
-    wait(q_out, sem2.at[n_dq])
+    wait(q_out.at[:, :, low], sem2.at[n_dqa])
+    wait(q_out.at[:, :, high], sem2.at[n_dqb])
     wait(v_out, sem2.at[n_dv])
     wait(k_out.at[:, :, low], sem2.at[n_dka])
     wait(k_out.at[:, :, high], sem2.at[n_dkb])
+
+
+def deliver(q_done, k_done, v_done, g_done, q_out, k_out, v_out, g_out, sem):
+    pairs = ((q_done, q_out), (k_done, k_out), (v_done, v_out))
+    copies = [
+        pltpu.make_async_copy(src.at[part], dst.at[part], sem.at[n, part])
+        for n, (src, dst) in enumerate(pairs)
+        for part in range(NY)
+    ]
+    for copy in copies:
+        copy.start()
+    g_out[...] = g_done[0, 0 : g_out.shape[0]]
+    for copy in copies:
+        copy.wait()
 
 
 def on_device(query_raw, key_raw, values, residuals, block_section, gain_query, gain_key):
@@ -264,35 +293,24 @@
     local_shape = query_raw.shape
     grid = (NY, NZ, 64, 128)
     vmem, dma = pltpu.VMEM, pltpu.SemaphoreType.DMA
-    block = functools.partial(vmem, dtype=BF)
-    full = jax.ShapeDtypeStruct(grid, BF)
     scratch = [
         vmem((NZ, NY, 64, 128), BF), vmem(grid, BF), vmem((2, 32, 32, 128), BF),
         *[vmem((3, 32, 16, 128), BF)] * 4,
         vmem(grid, BF), vmem(grid, BF), vmem(grid, BF),
         *[vmem((3, NY, NZ, 16, 128), BF)] * 4,
-        vmem((2048, 128), BF), vmem((128, 2048), BF),
-        vmem((16, 32, 128), F32), vmem((512, 128), BF),
-        vmem((2048, QB), F32), vmem((2048, QB), F32),
+        vmem((2048, 128), BF), vmem((4, QB, 128), BF), vmem((QB, 128), F32),
+        vmem((4, 2048, QB), F32), vmem((4, 2048, QB), BF), vmem((4, 128, QB), F32),
         vmem((2048, 128), F32), vmem((2048, 128), F32),
         vmem(grid, BF), vmem(grid, BF), vmem(grid, BF),
-        vmem((NZ, NY, 64, 128), BF), vmem((NZ, NY, 32, 128), BF), vmem((NY, NZ, 32, 128), BF), vmem(grid, BF),
+        *[vmem((NZ, NY, 32, 128), BF), vmem((NY, NZ, 32, 128), BF)] * 2, vmem(grid, BF),
         vmem((3, 8, 128), F32), vmem((NZ, 8, 128), F32), vmem((NY, 8, 128), F32), vmem((n_dp, 8, 128), F32),
-        dma((20,)), dma((20,)), dma((20,)), dma((20,)), dma((3,)), dma((3,)),
+        pltpu.SMEM((3,), jnp.int32), vmem((1, 128), F32), vmem((1, 128), F32),
+        dma((21,)), dma((21,)), dma((21,)), dma((21,)), dma((3,)), dma((3,)), dma((3,)),
     ]
     anywhere = pl.BlockSpec(memory_space=pl.ANY)
     inside = pl.BlockSpec(memory_space=pltpu.VMEM)
-    grad_q, grad_k, grad_v, gains = pl.pallas_call(
-        kernel,
-        out_shape=(full, full, full, jax.ShapeDtypeStruct((8, 128), F32)),
-        in_specs=[pl.BlockSpec(memory_space=pltpu.SMEM), inside, inside] + [anywhere] * 4,
-        out_specs=(anywhere, anywhere, anywhere, inside),
-        scratch_shapes=scratch,
-        compiler_params=pltpu.CompilerParams(
-            collective_id=0, has_side_effects=True, vmem_limit_bytes=48 << 20
-        ),
-        name="attention_backward",
-    )(
+    kept = pltpu.VMEM(grid, BF)
+    operands = (
         block_section,
         gain_query.reshape(1, 128),
         gain_key.reshape(1, 128),
@@ -301,8 +319,27 @@
         values.reshape(grid),
         residuals.reshape((3,) + grid),
     )
-    share = 256 // n_dp
-    grad_gains = lax.dynamic_slice(gains.reshape(-1), (lax.axis_index("dp") * share,), (share,))
+    done = pl.pallas_call(
+        kernel,
+        out_shape=(kept, kept, kept, pltpu.VMEM((8, 128), F32)),
+        in_specs=[anywhere] * 7,
+        out_specs=(anywhere, anywhere, anywhere, inside),
+        scratch_shapes=scratch,
+        compiler_params=pltpu.CompilerParams(
+            collective_id=0, has_side_effects=True, vmem_limit_bytes=56 << 20
+        ),
+        name="attention_backward",
+    )(*[pltpu.with_memory_space_constraint(operand, pltpu.HBM) for operand in operands])
+    full = jax.ShapeDtypeStruct(grid, BF)
+    grad_q, grad_k, grad_v, grad_gains = pl.pallas_call(
+        deliver,
+        out_shape=(full, full, full, jax.ShapeDtypeStruct((256 // n_dp,), F32)),
+        in_specs=[anywhere] * 3 + [inside],
+        out_specs=(anywhere, anywhere, anywhere, inside),
+        scratch_shapes=[dma((3, NY))],
+        compiler_params=pltpu.CompilerParams(vmem_limit_bytes=1 << 20),
+        name="deliver",
+    )(*done)
     return (
         grad_q.reshape(local_shape),
         grad_k.reshape(local_shape),

time: 159 us -> 142 us (0.89)
  the two profiles are of different devices: /device:TPU:5 before, /device:TPU:1 now
where the time goes in v1:
time: 142 us; the launch traced here: 139 us
  Pallas kernels  139 us (98%)
    pallas_call x1, Pallas kernels, on_device(): pl.pallas_call(kernel, out_shape=(kept, kept, kept, pltpu.VMEM((8, 128),...  137 us

profile of v1, /device:TPU:1, one launch (start us, length us, event | category | flops | bytes accessed | tf_op | source)
XLA Modules:
  0.0 139.4 jit_solution(939272023171855570)
XLA Ops:
  0.6 137.0 %attention_backward.1 = (bf16[4,8,64,128]{3,2,1,0:T(8,128)(2,1)S(1)}, bf16[4,8,64,128]{3,2,1,0:T(8,128)(2,1)S(1)}, bf16[4,8,64,128]{3,2,1,0:T(8,128)(2,1)S(1)}, f32[8,128]{1,0:T(8,128)S(1)}) custom-call(s32[3]{0:T(128)} %sec_in.1, f32[1,128]{1,0:T(1,128)} %bitcast.13, f32[1,128]{1,0:T(1,128)} %bitcast.14, bf16[4,8,64,128]{3,2,1,0:T(8,128)(2,1)} %bitcast.10, ...), custom_call_target="tpu_custom_call" | custom-call | tf_op jit(solution)/shard_map/attention_backward/pallas_call | solution.py:322
  137.6 1.7 %deliver.1 = (bf16[4,8,64,128]{3,2,1,0:T(8,128)(2,1)}, bf16[4,8,64,128]{3,2,1,0:T(8,128)(2,1)}, bf16[4,8,64,128]{3,2,1,0:T(8,128)(2,1)}, f32[16]{0:T(128)}) custom-call(bf16[4,8,64,128]{3,2,1,0:T(8,128)(2,1)S(1)} %get-tuple-element.12.q_done, bf16[4,8,64,128]{3,2,1,0:T(8,128)(2,1)S(1)} %get-tuple-element.13.k_done, ...), custom_call_target="tpu_custom_call" | custom-call | tf_op jit(solution)/shard_map/deliver/pallas_call | solution.py:334

commit v2 on v1

--- a/solution.py
+++ b/solution.py
@@ -34,7 +34,7 @@
     k_mid, v_mid, q_mid, r_mid0, r_mid1, r_mid2, r_mid3,
     k_land, v_land, q_land, r_land0, r_land1, r_land2, r_land3,
     kn, qn, do_f, probs, probs_b, mixed, dk_acc, dv_acc,
-    dq_stage, dk_stage, dv_stage, dq_mid_a, dq_mid_b, dk_mid_a, dk_mid_b, dv_mid,
+    dq_stage, dk_stage, dv_stage, dq_mid_a, dq_mid_b, dk_mid_a, dk_mid_b, dv_mid_a, dv_mid_b,
     g_part, g_z, g_y, g_d, sec, gain_q, gain_k,
     sem1, sem2, send1, send2, gsem, gsend, own,
 ):
@@ -59,8 +59,6 @@
         pl.semaphore_signal(barrier, 1, device_id=at_y(dy), device_id_type=MESH)
     for dd in range(1, n_dp):
         pl.semaphore_signal(barrier, 1, device_id={"dp": (dp + dd) % n_dp}, device_id_type=MESH)
-    pl.semaphore_wait(barrier, NZ - 1 + NY - 1 + n_dp - 1)
-
     def local(src, dst, sem):
         pltpu.make_async_copy(src, dst, sem).start()
 
@@ -75,13 +73,17 @@
     zo = (4, 3, 5, 2, 6, 1, 7)
     yo = (2, 1, 3)
 
+    def keep(n, path, src, mid):
+        if path == "a":
+            local(src.at[:, z], mid.at[z], sem1.at[n])
+        else:
+            local(src.at[y], mid.at[y], sem1.at[n])
+
     def first(n, path, src, mid):
         if path == "a":
-            local(src.at[:, z], mid.at[z], sem1.at[n])
             for dz in zo:
                 remote(src.at[:, (z + dz) % NZ], mid.at[z], send1.at[n], sem1.at[n], at_z(dz))
         else:
-            local(src.at[y], mid.at[y], sem1.at[n])
             for dy in yo:
                 remote(src.at[(y + dy) % NY], mid.at[y], send1.at[n], sem1.at[n], at_y(dy))
 
@@ -120,11 +122,14 @@
             )
     n_in = len(streams)
 
-    for n, (path, src, mid, land) in enumerate(streams):
-        first(n, path, src, mid)
     small = ((sec_in, sec), (gain_q_in, gain_q), (gain_k_in, gain_k))
     for n, (src, dst) in enumerate(small):
         local(src, dst, own.at[n])
+    for n, (path, src, mid, land) in enumerate(streams):
+        keep(n, path, src, mid)
+    pl.semaphore_wait(barrier, NZ - 1 + NY - 1 + n_dp - 1)
+    for n, (path, src, mid, land) in enumerate(streams):
+        first(n, path, src, mid)
     for n, (path, src, mid, land) in enumerate(streams):
         second(n, path, mid, land)
     for n, (src, dst) in enumerate(small):
@@ -158,7 +163,8 @@
 
     lax.fori_loop(0, 4, before, 0)
 
-    n_dqa, n_dqb, n_dv, n_dka, n_dkb = range(n_in, n_in + 5)
+    n_dqa, n_dqb, n_dva, n_dvb, n_dka, n_dkb = range(n_in, n_in + 6)
+    g_part[...] = jnp.zeros_like(g_part)
 
     def send_dq(c):
         local(dq_stage.at[c, z, low], dq_mid_a.at[z, c], sem1.at[n_dqa])
@@ -186,9 +192,6 @@
             def _():
                 for i in range(3):
                     wait(r_land[cc].at[i], sem2.at[4 + 3 * cc + i])
-                if cc == 3:
-                    for done in range(3):
-                        send_dq(done)
                 for r in range(32):
                     total = None
                     for i in range(3):
@@ -198,38 +201,49 @@
                     do_f[pl.ds(r, 16, stride=32), :] = total
 
         grad_out = do_f[...].astype(BF)
+        dv_acc[...] += dot(probs_b[c], grad_out, ((1,), (0,)))
+
+        @pl.when(c == 3)
+        def _():
+            dv_stage[...] = dv_acc[...].astype(BF).reshape(NY, NZ, 64, 128)
+            for n, path, rows, mid in ((n_dva, "a", low, dv_mid_a), (n_dvb, "b", high, dv_mid_b)):
+                first(n, path, dv_stage.at[:, :, rows], mid)
+                keep(n, path, dv_stage.at[:, :, rows], mid)
+
         centre = jnp.sum(grad_out.astype(F32).T * mixed[c], axis=0, keepdims=True)
         grad_probs = dot(v_land[...].reshape(2048, 128), grad_out, ((1,), (1,)))
         grad_scores = (probs[c] * (grad_probs - centre)).astype(BF)
         dk_acc[...] += dot(grad_scores, qn[c], ((1,), (0,)))
-        dv_acc[...] += dot(probs_b[c], grad_out, ((1,), (0,)))
+
+        @pl.when(c == 3)
+        def _():
+            part_k = jnp.zeros((1, 128), F32)
+            for t in range(NY):
+                unit, inverse = normalize(k_land[t].reshape(512, 128).astype(F32))
+                grad_norm = dk_acc[pl.ds(512 * t, 512), :] * scale
+                part_k = part_k + jnp.sum(grad_norm * unit, axis=0, keepdims=True)
+                out = restore(unit, inverse, grad_norm, gain_k[...]).astype(BF)
+                dk_stage[t] = out.reshape(NZ, 64, 128)
+            g_part[0, 1:2, :] = part_k
+            for n, path, rows, mid in ((n_dka, "a", low, dk_mid_a), (n_dkb, "b", high, dk_mid_b)):
+                first(n, path, dk_stage.at[:, :, rows], mid)
+                keep(n, path, dk_stage.at[:, :, rows], mid)
+
         grad_norm = dot(kn[...], grad_scores, ((0,), (0,))).T * scale
         unit, inverse = normalize(q_land[c].reshape(QB, 128).astype(F32))
         out = restore(unit, inverse, grad_norm, gain_q[...]).astype(BF)
         dq_stage[c] = out.reshape(NZ, 64, 128)
+        send_dq(c)
         return part_q + jnp.sum(grad_norm * unit, axis=0, keepdims=True)
 
-    part_q = lax.fori_loop(0, 4, after, jnp.zeros((1, 128), F32))
-    send_dq(3)
-
-    for t in range(NY):
-        dv_stage[t] = dv_acc[pl.ds(512 * t, 512), :].astype(BF).reshape(NZ, 64, 128)
-    first(n_dv, "b", dv_stage, dv_mid)
-    part_k = jnp.zeros((1, 128), F32)
-    for t in range(NY):
-        unit, inverse = normalize(k_land[t].reshape(512, 128).astype(F32))
-        grad_norm = dk_acc[pl.ds(512 * t, 512), :] * scale
-        part_k = part_k + jnp.sum(grad_norm * unit, axis=0, keepdims=True)
-        out = restore(unit, inverse, grad_norm, gain_k[...]).astype(BF)
-        dk_stage[t] = out.reshape(NZ, 64, 128)
-
-    g_part[0, :, :] = jnp.concatenate([part_q, part_k, jnp.zeros((6, 128), F32)], axis=0)
+    g_part[0, 0:1, :] = lax.fori_loop(0, 4, after, jnp.zeros((1, 128), F32))
+
     local(g_part.at[0], g_z.at[z], gsem.at[0])
     for dz in zo:
         remote(g_part.at[0], g_z.at[z], gsend.at[0], gsem.at[0], at_z(dz))
 
-    first(n_dka, "a", dk_stage.at[:, :, low], dk_mid_a)
-    first(n_dkb, "b", dk_stage.at[:, :, high], dk_mid_b)
+    second(n_dva, "a", dv_mid_a, v_out.at[:, :, low])
+    second(n_dvb, "b", dv_mid_b, v_out.at[:, :, high])
 
     wait(g_z, gsem.at[0])
     g_part[1, :, :] = jnp.sum(g_z[...], axis=0)
@@ -237,8 +251,8 @@
     for dy in yo:
         remote(g_part.at[1], g_y.at[y], gsend.at[1], gsem.at[1], at_y(dy))
 
-    second(n_dqa, "a", dq_mid_a, q_out.at[:, :, low])
-    second(n_dqb, "b", dq_mid_b, q_out.at[:, :, high])
+    second(n_dka, "a", dk_mid_a, k_out.at[:, :, low])
+    second(n_dkb, "b", dk_mid_b, k_out.at[:, :, high])
 
     wait(g_y, gsem.at[1])
     g_part[2, :, :] = jnp.sum(g_y[...], axis=0)
@@ -246,9 +260,8 @@
     for dd in range(1, n_dp):
         remote(g_part.at[2], g_d.at[dp], gsend.at[2], gsem.at[2], {"dp": (dp + dd) % n_dp})
 
-    second(n_dv, "b", dv_mid, v_out)
-    second(n_dka, "a", dk_mid_a, k_out.at[:, :, low])
-    second(n_dkb, "b", dk_mid_b, k_out.at[:, :, high])
+    second(n_dqa, "a", dq_mid_a, q_out.at[:, :, low])
+    second(n_dqb, "b", dq_mid_b, q_out.at[:, :, high])
 
     wait(g_d, gsem.at[2])
     sums = jnp.sum(g_d[...], axis=0)
@@ -261,7 +274,8 @@
         sent(n, path, mid)
     sent(n_dqa, "a", dq_mid_a)
     sent(n_dqb, "b", dq_mid_b)
-    sent(n_dv, "b", dv_mid)
+    sent(n_dva, "a", dv_mid_a)
+    sent(n_dvb, "b", dv_mid_b)
     sent(n_dka, "a", dk_mid_a)
     sent(n_dkb, "b", dk_mid_b)
     wait(g_z.at[pl.ds(0, NZ - 1)], gsend.at[0])
@@ -269,7 +283,8 @@
     wait(g_d.at[pl.ds(0, n_dp - 1)], gsend.at[2])
     wait(q_out.at[:, :, low], sem2.at[n_dqa])
     wait(q_out.at[:, :, high], sem2.at[n_dqb])
-    wait(v_out, sem2.at[n_dv])
+    wait(v_out.at[:, :, low], sem2.at[n_dva])
+    wait(v_out.at[:, :, high], sem2.at[n_dvb])
     wait(k_out.at[:, :, low], sem2.at[n_dka])
     wait(k_out.at[:, :, high], sem2.at[n_dkb])
 
@@ -302,10 +317,10 @@
         vmem((4, 2048, QB), F32), vmem((4, 2048, QB), BF), vmem((4, 128, QB), F32),
         vmem((2048, 128), F32), vmem((2048, 128), F32),
         vmem(grid, BF), vmem(grid, BF), vmem(grid, BF),
-        *[vmem((NZ, NY, 32, 128), BF), vmem((NY, NZ, 32, 128), BF)] * 2, vmem(grid, BF),
+        *[vmem((NZ, NY, 32, 128), BF), vmem((NY, NZ, 32, 128), BF)] * 3,
         vmem((3, 8, 128), F32), vmem((NZ, 8, 128), F32), vmem((NY, 8, 128), F32), vmem((n_dp, 8, 128), F32),
         pltpu.SMEM((3,), jnp.int32), vmem((1, 128), F32), vmem((1, 128), F32),
-        dma((21,)), dma((21,)), dma((21,)), dma((21,)), dma((3,)), dma((3,)), dma((3,)),
+        dma((22,)), dma((22,)), dma((22,)), dma((22,)), dma((3,)), dma((3,)), dma((3,)),
     ]
     anywhere = pl.BlockSpec(memory_space=pl.ANY)
     inside = pl.BlockSpec(memory_space=pltpu.VMEM)

time: 142 us -> 132 us (0.930); the launches traced: 139 us -> 132 us
  Pallas kernels: 139 us -> 131 us
    pallas_call x1, Pallas kernels: 137 us -> 129 us  [on_device(): pl.pallas_call(kernel, out_shape=(kept, kept, kept, pltpu.VMEM((8, 128),...]
where the time goes in v2:
time: 132 us
  Pallas kernels  131 us (99%)
    pallas_call x1, Pallas kernels, on_device(): pl.pallas_call(kernel, out_shape=(kept, kept, kept, pltpu.VMEM((8, 128),...  129 us

profile of v2, /device:TPU:1, one launch (start us, length us, event | category | flops | bytes accessed | tf_op | source)
XLA Modules:
  0.0 131.8 jit_solution(3101553487550936095)
XLA Ops:
  0.6 129.4 %attention_backward.1 = (bf16[4,8,64,128]{3,2,1,0:T(8,128)(2,1)S(1)}, bf16[4,8,64,128]{3,2,1,0:T(8,128)(2,1)S(1)}, bf16[4,8,64,128]{3,2,1,0:T(8,128)(2,1)S(1)}, f32[8,128]{1,0:T(8,128)S(1)}) custom-call(s32[3]{0:T(128)} %sec_in.1, f32[1,128]{1,0:T(1,128)} %bitcast.13, f32[1,128]{1,0:T(1,128)} %bitcast.14, bf16[4,8,64,128]{3,2,1,0:T(8,128)(2,1)} %bitcast.10, ...), custom_call_target="tpu_custom_call" | custom-call | tf_op jit(solution)/shard_map/attention_backward/pallas_call | solution.py:337
  130.1 1.7 %deliver.1 = (bf16[4,8,64,128]{3,2,1,0:T(8,128)(2,1)}, bf16[4,8,64,128]{3,2,1,0:T(8,128)(2,1)}, bf16[4,8,64,128]{3,2,1,0:T(8,128)(2,1)}, f32[16]{0:T(128)}) custom-call(bf16[4,8,64,128]{3,2,1,0:T(8,128)(2,1)S(1)} %get-tuple-element.12.q_done, bf16[4,8,64,128]{3,2,1,0:T(8,128)(2,1)S(1)} %get-tuple-element.13.k_done, ...), custom_call_target="tpu_custom_call" | custom-call | tf_op jit(solution)/shard_map/deliver/pallas_call | solution.py:349

commit v3 on v2

--- a/solution.py
+++ b/solution.py
@@ -107,13 +107,17 @@
             wait(mid.at[:, pl.ds(0, NZ - 1)], send2.at[n])
 
     low, high = pl.ds(0, 32), pl.ds(32, 32)
-    streams = [
-        ("a", k_in, k_mid, k_land),
-        ("b", v_in, v_mid, v_land),
-        ("a", q_in.at[:, :, low], q_mid.at[0].reshape(NZ, NY, 32, 128), q_land.at[:, :, low]),
-        ("b", q_in.at[:, :, high], q_mid.at[1].reshape(NY, NZ, 32, 128), q_land.at[:, :, high]),
-    ]
+    streams = []
+    groups = []
+    for half, rows in enumerate((low, high)):
+        streams.append(("b", v_in.at[:, :, rows], v_mid.at[half], v_land.at[:, :, rows]))
+        streams.append(("a", k_in.at[:, :, rows], k_mid.at[half], k_land.at[:, :, rows]))
+        groups.append((2 * half, 2 * half + 1))
+    streams.append(("b", q_in.at[:, :, high], q_mid.at[1].reshape(NY, NZ, 32, 128), q_land.at[:, :, high]))
+    streams.append(("a", q_in.at[:, :, low], q_mid.at[0].reshape(NZ, NY, 32, 128), q_land.at[:, :, low]))
+    groups.append((4, 5))
     for c in range(4):
+        groups.append(tuple(len(streams) + i for i in range(3)))
         for i in range(3):
             path = ("a", "b", "ab"[c % 2])[i]
             shape = (NZ, NY, 16, 128) if path == "a" else (NY, NZ, 16, 128)
@@ -122,28 +126,54 @@
             )
     n_in = len(streams)
 
+    def first_legs(group):
+        for n in groups[group]:
+            path, src, mid, _ = streams[n]
+            first(n, path, src, mid)
+
+    def second_legs(group):
+        for n in groups[group]:
+            path, _, mid, land = streams[n]
+            second(n, path, mid, land)
+
+    def landed(group):
+        for n in groups[group]:
+            wait(streams[n][3], sem2.at[n])
+
+    def own_blocks(group):
+        for n in groups[group]:
+            path, src, mid, _ = streams[n]
+            keep(n, path, src, mid)
+
+    for group in range(3):
+        own_blocks(group)
+    pl.semaphore_wait(barrier, NZ - 1 + NY - 1 + n_dp - 1)
+    for group in range(5):
+        first_legs(group)
+    for group in range(3, 7):
+        own_blocks(group)
     small = ((sec_in, sec), (gain_q_in, gain_q), (gain_k_in, gain_k))
     for n, (src, dst) in enumerate(small):
         local(src, dst, own.at[n])
-    for n, (path, src, mid, land) in enumerate(streams):
-        keep(n, path, src, mid)
-    pl.semaphore_wait(barrier, NZ - 1 + NY - 1 + n_dp - 1)
-    for n, (path, src, mid, land) in enumerate(streams):
-        first(n, path, src, mid)
-    for n, (path, src, mid, land) in enumerate(streams):
-        second(n, path, mid, land)
+    g_part[...] = jnp.zeros_like(g_part)
+    dk_acc[...] = jnp.zeros_like(dk_acc)
+    dv_acc[...] = jnp.zeros_like(dv_acc)
     for n, (src, dst) in enumerate(small):
         pltpu.make_async_copy(src, dst, own.at[n]).wait()
-
-    wait(k_land, sem2.at[0])
+    second_legs(0)
+    first_legs(5)
+    second_legs(1)
+    first_legs(6)
+    second_legs(2)
+
+    landed(0)
+    landed(1)
     for t in range(NY):
         unit, _ = normalize(k_land[t].reshape(512, 128).astype(F32))
         kn[pl.ds(512 * t, 512), :] = (unit * gain_k[...]).astype(BF)
-    dk_acc[...] = jnp.zeros_like(dk_acc)
-    dv_acc[...] = jnp.zeros_like(dv_acc)
-    wait(v_land, sem2.at[1])
-    wait(q_land.at[:, :, low], sem2.at[2])
-    wait(q_land.at[:, :, high], sem2.at[3])
+    second_legs(3)
+    second_legs(4)
+    landed(2)
 
     def before(c, carry):
         unit, _ = normalize(q_land[c].reshape(QB, 128).astype(F32))
@@ -161,10 +191,12 @@
         mixed[c] = dot(held, upper, ((0,), (0,))) + dot(held, lower, ((0,), (0,)))
         return carry
 
-    lax.fori_loop(0, 4, before, 0)
+    lax.fori_loop(0, 2, before, 0)
+    second_legs(5)
+    lax.fori_loop(2, 4, before, 0)
+    second_legs(6)
 
     n_dqa, n_dqb, n_dva, n_dvb, n_dka, n_dkb = range(n_in, n_in + 6)
-    g_part[...] = jnp.zeros_like(g_part)
 
     def send_dq(c):
         local(dq_stage.at[c, z, low], dq_mid_a.at[z, c], sem1.at[n_dqa])
@@ -190,8 +222,7 @@
 
             @pl.when(c == cc)
             def _():
-                for i in range(3):
-                    wait(r_land[cc].at[i], sem2.at[4 + 3 * cc + i])
+                landed(3 + cc)
                 for r in range(32):
                     total = None
                     for i in range(3):
@@ -254,14 +285,14 @@
     second(n_dka, "a", dk_mid_a, k_out.at[:, :, low])
     second(n_dkb, "b", dk_mid_b, k_out.at[:, :, high])
 
+    second(n_dqa, "a", dq_mid_a, q_out.at[:, :, low])
+    second(n_dqb, "b", dq_mid_b, q_out.at[:, :, high])
+
     wait(g_y, gsem.at[1])
     g_part[2, :, :] = jnp.sum(g_y[...], axis=0)
     local(g_part.at[2], g_d.at[dp], gsem.at[2])
     for dd in range(1, n_dp):
         remote(g_part.at[2], g_d.at[dp], gsend.at[2], gsem.at[2], {"dp": (dp + dd) % n_dp})
-
-    second(n_dqa, "a", dq_mid_a, q_out.at[:, :, low])
-    second(n_dqb, "b", dq_mid_b, q_out.at[:, :, high])
 
     wait(g_d, gsem.at[2])
     sums = jnp.sum(g_d[...], axis=0)
@@ -309,7 +340,7 @@
     grid = (NY, NZ, 64, 128)
     vmem, dma = pltpu.VMEM, pltpu.SemaphoreType.DMA
     scratch = [
-        vmem((NZ, NY, 64, 128), BF), vmem(grid, BF), vmem((2, 32, 32, 128), BF),
+        vmem((2, NZ, NY, 32, 128), BF), vmem((2, NY, NZ, 32, 128), BF), vmem((2, 32, 32, 128), BF),
         *[vmem((3, 32, 16, 128), BF)] * 4,
         vmem(grid, BF), vmem(grid, BF), vmem(grid, BF),
         *[vmem((3, NY, NZ, 16, 128), BF)] * 4,
@@ -320,7 +351,7 @@
         *[vmem((NZ, NY, 32, 128), BF), vmem((NY, NZ, 32, 128), BF)] * 3,
         vmem((3, 8, 128), F32), vmem((NZ, 8, 128), F32), vmem((NY, 8, 128), F32), vmem((n_dp, 8, 128), F32),
         pltpu.SMEM((3,), jnp.int32), vmem((1, 128), F32), vmem((1, 128), F32),
-        dma((22,)), dma((22,)), dma((22,)), dma((22,)), dma((3,)), dma((3,)), dma((3,)),
+        dma((24,)), dma((24,)), dma((24,)), dma((24,)), dma((3,)), dma((3,)), dma((3,)),
     ]
     anywhere = pl.BlockSpec(memory_space=pl.ANY)
     inside = pl.BlockSpec(memory_space=pltpu.VMEM)

time: 132 us -> 130 us (0.985)
  Pallas kernels: 131 us -> 129 us
    pallas_call x1, Pallas kernels: 129 us -> 128 us  [on_device(): pl.pallas_call(kernel, out_shape=(kept, kept, kept, pltpu.VMEM((8, 128),...]
where the time goes in v3:
time: 130 us
  Pallas kernels  129 us (99%)
    pallas_call x1, Pallas kernels, on_device(): pl.pallas_call(kernel, out_shape=(kept, kept, kept, pltpu.VMEM((8, 128),...  128 us

profile of v3, /device:TPU:1, one launch (start us, length us, event | category | flops | bytes accessed | tf_op | source)
XLA Modules:
  0.0 130.3 jit_solution(14207964233026204955)
XLA Ops:
  0.6 127.7 %attention_backward.1 = (bf16[4,8,64,128]{3,2,1,0:T(8,128)(2,1)S(1)}, bf16[4,8,64,128]{3,2,1,0:T(8,128)(2,1)S(1)}, bf16[4,8,64,128]{3,2,1,0:T(8,128)(2,1)S(1)}, f32[8,128]{1,0:T(8,128)S(1)}) custom-call(s32[3]{0:T(128)} %sec_in.1, f32[1,128]{1,0:T(1,128)} %bitcast.13, f32[1,128]{1,0:T(1,128)} %bitcast.14, bf16[4,8,64,128]{3,2,1,0:T(8,128)(2,1)} %bitcast.10, ...), custom_call_target="tpu_custom_call" | custom-call | tf_op jit(solution)/shard_map/attention_backward/pallas_call | solution.py:368
  128.4 1.7 %deliver.1 = (bf16[4,8,64,128]{3,2,1,0:T(8,128)(2,1)}, bf16[4,8,64,128]{3,2,1,0:T(8,128)(2,1)}, bf16[4,8,64,128]{3,2,1,0:T(8,128)(2,1)}, f32[16]{0:T(128)}) custom-call(bf16[4,8,64,128]{3,2,1,0:T(8,128)(2,1)S(1)} %get-tuple-element.12.q_done, bf16[4,8,64,128]{3,2,1,0:T(8,128)(2,1)S(1)} %get-tuple-element.13.k_done, ...), custom_call_target="tpu_custom_call" | custom-call | tf_op jit(solution)/shard_map/deliver/pallas_call | solution.py:380

commit v4 on v3

--- a/solution.py
+++ b/solution.py
@@ -191,9 +191,9 @@
         mixed[c] = dot(held, upper, ((0,), (0,))) + dot(held, lower, ((0,), (0,)))
         return carry
 
-    lax.fori_loop(0, 2, before, 0)
+    lax.fori_loop(0, 1, before, 0)
     second_legs(5)
-    lax.fori_loop(2, 4, before, 0)
+    lax.fori_loop(1, 4, before, 0)
     second_legs(6)
 
     n_dqa, n_dqb, n_dva, n_dvb, n_dka, n_dkb = range(n_in, n_in + 6)

time: 130 us -> 131 us (level)
  no operation moved by 1% of the time
where the time goes in v4:
time: 131 us; the launch traced here: 130 us
  Pallas kernels  129 us (98%)
    pallas_call x1, Pallas kernels, on_device(): pl.pallas_call(kernel, out_shape=(kept, kept, kept, pltpu.VMEM((8, 128),...  128 us

profile of v4, /device:TPU:1, one launch (start us, length us, event | category | flops | bytes accessed | tf_op | source)
XLA Modules:
  0.0 130.3 jit_solution(8126201782925289913)
XLA Ops:
  0.6 127.7 %attention_backward.1 = (bf16[4,8,64,128]{3,2,1,0:T(8,128)(2,1)S(1)}, bf16[4,8,64,128]{3,2,1,0:T(8,128)(2,1)S(1)}, bf16[4,8,64,128]{3,2,1,0:T(8,128)(2,1)S(1)}, f32[8,128]{1,0:T(8,128)S(1)}) custom-call(s32[3]{0:T(128)} %sec_in.1, f32[1,128]{1,0:T(1,128)} %bitcast.13, f32[1,128]{1,0:T(1,128)} %bitcast.14, bf16[4,8,64,128]{3,2,1,0:T(8,128)(2,1)} %bitcast.10, ...), custom_call_target="tpu_custom_call" | custom-call | tf_op jit(solution)/shard_map/attention_backward/pallas_call | solution.py:368
  128.4 1.7 %deliver.1 = (bf16[4,8,64,128]{3,2,1,0:T(8,128)(2,1)}, bf16[4,8,64,128]{3,2,1,0:T(8,128)(2,1)}, bf16[4,8,64,128]{3,2,1,0:T(8,128)(2,1)}, f32[16]{0:T(128)}) custom-call(bf16[4,8,64,128]{3,2,1,0:T(8,128)(2,1)S(1)} %get-tuple-element.12.q_done, bf16[4,8,64,128]{3,2,1,0:T(8,128)(2,1)S(1)} %get-tuple-element.13.k_done, ...), custom_call_target="tpu_custom_call" | custom-call | tf_op jit(solution)/shard_map/deliver/pallas_call | solution.py:380
